TPU v7x, 128 devices: a whole 4x4x4 slice. The times are simulated.
128 devices in a mesh: outer: 8 (over x, core), inner: 16 (over z, y).
Axes of the slice: x: 4, y: 4, z: 4, core: 2. Of those that a mesh axis runs over, the one named last changes fastest.
Arguments:
- query_vec: bfloat16 [131072, 256], P(('outer', 'inner')), may hold values from -40 to 40
- key_vec: bfloat16 [131072, 256], P(('outer', 'inner')), may hold values from -9 to 9
- value_vec: bfloat16 [131072, 256], P(('outer', 'inner')), may hold values from -6 to 6
- grad_out: bfloat16 [131072, 256], P(('outer', 'inner')), may hold values from -6 to 6
- chosen: int32 [128, 3], replicated, may hold values from 0 to 127, as said below
- layout: int32 [16], replicated, may hold values from 0 to 15, each once
Outputs:
- grad_query: bfloat16 [131072, 256], P(('outer', 'inner'))
- grad_key: bfloat16 [131072, 256], P(('outer', 'inner'))
- grad_value: bfloat16 [131072, 256], P(('outer', 'inner'))
Inputs may be any that keep to these rules, and one draw needn't show every extreme that they name: `chosen`: row b lists the blocks picked by query block b's gate among all earlier blocks of the sequence: min(3, b) distinct blocks below b, and b itself in the remaining slots.
All inputs are finite; a program needn't handle non-finite values.
Results may differ from a plain program's by a relative error of at most 0.02.
Values may be sent and summed in bfloat16 or wider, within the bound.
A program may use at most 128 MiB of HBM per device.

v0:
```python
import functools
import math

import jax
import jax.numpy as jnp
from jax import lax
from jax.experimental import pallas as pl
from jax.experimental.pallas import tpu as pltpu
from jax.sharding import PartitionSpec as P

HEADS = 2
HD = 128
TOPK = 3
OWN = TOPK
TILE = 16
CHUNK = 256
MESH = pl.DeviceIdType.MESH
F32 = jnp.float32
BF16 = jnp.bfloat16
SCALE = 1.0 / math.sqrt(HD)
EXP2_SCALE = SCALE * math.log2(math.e)


def dot(a, b):
    return jnp.dot(a, b, preferred_element_type=F32)


def fold(x, op):
    return op(x.reshape(x.shape[0] // 8, 8, x.shape[1]), axis=0)


def compute_head(h, picked, q, g, kv, kt, s_scr, dp_scr, dqt, dk, dv, gq_ref):
    length = q.shape[1]
    blocks = length // CHUNK

    for t in range(TOPK + 1):
        kt[t] = kv[h, t, :length].T
    dk[h] = jnp.zeros(dk.shape[1:], F32)
    dv[h] = jnp.zeros(dv.shape[1:], F32)

    def rows(t, b, base=0):
        return kv[h, t, pl.ds(pl.multiple_of(base + b * CHUNK, CHUNK), CHUNK)]

    def chunk(j, carry):
        here = pl.ds(pl.multiple_of(j * CHUNK, CHUNK), CHUNK)
        qc, gc = q[h, here], g[h, here]
        qtc, gtc = qc.T, gc.T
        low = jnp.full((8, CHUNK), -jnp.inf, F32)

        def scores(t, b, m):
            s = dot(rows(t, b), qtc)
            s_scr[t * blocks + b] = s
            return jnp.maximum(m, fold(s, jnp.max))

        def far_max(t, m):
            mt = low
            for b in range(blocks):
                mt = scores(t, b, mt)
            return jnp.maximum(m, jnp.where(picked(t), mt, -jnp.inf))

        m = lax.fori_loop(0, TOPK, far_max, low)
        m = lax.fori_loop(0, j, lambda b, m: scores(OWN, b, m), m)
        s = dot(rows(OWN, j), qtc)
        at = lambda d: lax.broadcasted_iota(jnp.int32, (CHUNK, CHUNK), d)
        s = jnp.where(at(0) <= at(1), s, -jnp.inf)
        s_scr[OWN * blocks + j] = s
        m = jnp.maximum(m, fold(s, jnp.max))
        top = jnp.max(m, axis=0, keepdims=True) * EXP2_SCALE

        def weigh(t, b, shift, sums):
            total, mixed = sums
            e = jnp.exp2(s_scr[t * blocks + b] * EXP2_SCALE - shift)
            dp = dot(rows(t, b, length), gtc)
            s_scr[t * blocks + b] = e
            dp_scr[t * blocks + b] = dp
            return total + fold(e, jnp.sum), mixed + fold(e * dp, jnp.sum)

        def far_weigh(t, sums):
            shift = jnp.where(picked(t), top, jnp.inf)
            for b in range(blocks):
                sums = weigh(t, b, shift, sums)
            return sums

        zero = jnp.zeros((8, CHUNK), F32)
        sums = lax.fori_loop(0, TOPK, far_weigh, (zero, zero))
        sums = lax.fori_loop(0, j + 1, lambda b, s: weigh(OWN, b, top, s), sums)
        inverse = 1.0 / jnp.sum(sums[0], axis=0, keepdims=True)
        delta = jnp.sum(sums[1], axis=0, keepdims=True) * inverse

        dqt[...] = jnp.zeros(dqt.shape, F32)

        def grads(t, b):
            p = s_scr[t * blocks + b] * inverse
            ds = (p * (dp_scr[t * blocks + b] - delta)).astype(BF16)
            there = pl.ds(pl.multiple_of(b * CHUNK, CHUNK), CHUNK)
            dv[h, t, there] += dot(p.astype(BF16), gc)
            dk[h, t, there] += dot(ds, qc)
            dqt[...] += dot(kt[t, :, there], ds)

        def far_grads(t, c):
            for b in range(blocks):
                grads(t, b)
            return c

        lax.fori_loop(0, TOPK, far_grads, 0)
        lax.fori_loop(0, j + 1, lambda b, c: (grads(OWN, b), c)[1], 0)
        gq_ref[here, h * HD : (h + 1) * HD] = (dqt[...].T * SCALE).astype(BF16)
        return carry

    lax.fori_loop(0, blocks, chunk, 0)


def kernel(
    n_outer, n_inner,
    chosen, layout, q_in, k_in, v_in, g_in,
    gq_ref, gk_ref, gv_ref,
    inverse, wanted, hot_rows, hot, q, g, kv, kt, s_scr, dp_scr, dqt, dk, dv,
    relay0, relay1, outgoing, terms, landed, wide, summed, back,
    in_sem, send_sem, recv_sem,
):
    devices = n_outer * n_inner
    relay = (relay0, relay1)
    my_outer, my_inner = lax.axis_index("outer"), lax.axis_index("inner")
    me = my_outer * n_inner + my_inner
    length = q.shape[1]

    def peer(s):
        o = lax.rem(my_outer + lax.div(s, n_inner), n_outer)
        i = lax.rem(my_inner + lax.rem(s, n_inner), n_inner)
        return o * n_inner + i, (o, i)

    barrier = pltpu.get_barrier_semaphore()

    def greet(s, c):
        pl.semaphore_signal(barrier, inc=1, device_id=peer(s)[1], device_id_type=MESH)
        return c

    lax.fori_loop(1, devices, greet, 0)

    loads = []
    for h in range(HEADS):
        cols = pl.ds(h * HD, HD)
        for src, dst in (
            (k_in, kv.at[h, OWN, pl.ds(0, length)]),
            (v_in, kv.at[h, OWN, pl.ds(length, length)]),
            (q_in, q.at[h]),
            (g_in, g.at[h]),
        ):
            copy = pltpu.make_async_copy(src.at[:, cols], dst, in_sem.at[len(loads)])
            copy.start()
            loads.append(copy)

    def invert(p, c):
        inverse[p] = sum(jnp.where(layout[j] == p, j, 0) for j in range(n_inner))
        return c

    lax.fori_loop(0, n_inner, invert, 0)
    lane = lax.broadcasted_iota(jnp.int32, (1, devices), 1)

    def want(r, c):
        block = lax.div(r, n_inner) * n_inner + layout[lax.rem(r, n_inner)]
        for t in range(TOPK):
            picked = chosen[block, t]
            row = lax.div(picked, n_inner) * n_inner + inverse[lax.rem(picked, n_inner)]
            wanted[r * TOPK + t] = row
            hot_rows[pl.ds(r * TOPK + t, 1), :] = jnp.where(lane == row, 1.0, 0.0)
        return c

    lax.fori_loop(0, devices, want, 0)
    hot[...] = hot_rows[...].T.astype(BF16)
    my_block = my_outer * n_inner + layout[my_inner]

    def picked(t):
        return chosen[my_block, t] < my_block

    for copy in loads:
        copy.wait()
    pl.semaphore_wait(barrier, devices - 1)

    def exchange(phase, src_of, dst):
        send, recv = send_sem.at[phase], recv_sem.at[phase]
        pltpu.make_async_copy(src_of(me), dst, recv).start()

        def go(s, c):
            r, where = peer(s)
            pltpu.make_async_remote_copy(
                src_ref=src_of(r), dst_ref=dst, send_sem=send, recv_sem=recv,
                device_id=where, device_id_type=MESH,
            ).start()
            return c

        lax.fori_loop(1, devices, go, 0)

    def arrived(phase, whole):
        pltpu.make_async_copy(whole, whole, recv_sem.at[phase]).wait()

    def place(r):
        return pl.ds(pl.multiple_of(r * TILE, TILE), TILE)

    far = lambda h: kv.at[h, pl.ds(0, TOPK)]

    for h in range(HEADS):
        exchange(h, lambda r: kv.at[h, OWN, place(r)], relay[h].at[me])

    for h in range(HEADS):
        arrived(h, relay[h])

        def pick(r, c):
            for t in range(TOPK):
                outgoing[h, r, t] = relay[h][wanted[r * TOPK + t]]
            return c

        lax.fori_loop(0, devices, pick, 0)
        exchange(2 + h, lambda r: outgoing.at[h, r], kv.at[h, pl.ds(0, TOPK), place(me)])

    for h in range(HEADS):
        arrived(2 + h, far(h))
        compute_head(h, picked, q, g, kv, kt, s_scr, dp_scr, dqt, dk, dv, gq_ref)
        for t in range(TOPK):
            terms[h, t, :length] = dk[h, t].astype(BF16)
            terms[h, t, length:] = dv[h, t].astype(BF16)
        exchange(4 + h, lambda r: terms.at[h, :, place(r)], landed.at[h, me])

    for h in range(HEADS):
        arrived(4 + h, landed.at[h])

        def widen(r, c):
            wide[pl.ds(r * TOPK * TILE, TOPK * TILE)] = (
                landed[h, r].astype(F32).reshape(TOPK * TILE, HD)
            )
            return c

        lax.fori_loop(0, devices, widen, 0)
        sums = []
        for s in range(TILE):
            part = wide[pl.ds(s, devices * TOPK, TILE), :].astype(BF16)
            sums.append(dot(hot[...], part))
        for s in range(TILE):
            wide[pl.ds(s, devices, TILE), :] = sums[s]
        summed[h] = wide[: devices * TILE].astype(BF16)
        exchange(6 + h, lambda r: summed.at[h, place(r)], back.at[h, place(me)])

    for h in range(HEADS):
        arrived(6 + h, back.at[h])
        cols = pl.ds(h * HD, HD)
        gk_ref[:, cols] = ((dk[h, OWN] + back[h, :length].astype(F32)) * SCALE).astype(BF16)
        gv_ref[:, cols] = (dv[h, OWN] + back[h, length:].astype(F32)).astype(BF16)

    def sent(phase, part):
        pltpu.make_async_copy(part, part, send_sem.at[phase]).wait()

    for h in range(HEADS):
        sent(h, relay[h].at[pl.ds(1, devices - 1)])
        sent(2 + h, outgoing.at[h, pl.ds(1, devices - 1)])
        sent(4 + h, landed.at[h, pl.ds(1, devices - 1)])
        sent(6 + h, summed.at[h, pl.ds(TILE, (devices - 1) * TILE)])


def on_device(query_vec, key_vec, value_vec, grad_out, chosen, layout):
    n_outer, n_inner = lax.axis_size("outer"), lax.axis_size("inner")
    devices = n_outer * n_inner
    length, width = query_vec.shape
    blocks = length // CHUNK
    out = jax.ShapeDtypeStruct((length, width), BF16)
    scratch = [
        pltpu.SMEM((n_inner,), jnp.int32),
        pltpu.SMEM((devices * TOPK,), jnp.int32),
        pltpu.VMEM((devices * TOPK, devices), F32),
        pltpu.VMEM((devices, devices * TOPK), BF16),
        pltpu.VMEM((HEADS, length, HD), BF16),
        pltpu.VMEM((HEADS, length, HD), BF16),
        pltpu.VMEM((HEADS, TOPK + 1, 2 * length, HD), BF16),
        pltpu.VMEM((TOPK + 1, HD, length), BF16),
        pltpu.VMEM(((TOPK + 1) * blocks, CHUNK, CHUNK), F32),
        pltpu.VMEM(((TOPK + 1) * blocks, CHUNK, CHUNK), F32),
        pltpu.VMEM((HD, CHUNK), F32),
        pltpu.VMEM((HEADS, TOPK + 1, length, HD), F32),
        pltpu.VMEM((HEADS, TOPK + 1, length, HD), F32),
        pltpu.VMEM((devices, TILE, HD), BF16),
        pltpu.VMEM((devices, TILE, HD), BF16),
        pltpu.VMEM((HEADS, devices, TOPK, TILE, HD), BF16),
        pltpu.VMEM((HEADS, TOPK, 2 * length, HD), BF16),
        pltpu.VMEM((HEADS, devices, TOPK, TILE, HD), BF16),
        pltpu.VMEM((devices * TOPK * TILE, HD), F32),
        pltpu.VMEM((HEADS, devices * TILE, HD), BF16),
        pltpu.VMEM((HEADS, devices * TILE, HD), BF16),
        pltpu.SemaphoreType.DMA((4 * HEADS,)),
        pltpu.SemaphoreType.DMA((4 * HEADS,)),
        pltpu.SemaphoreType.DMA((4 * HEADS,)),
    ]
    return pl.pallas_call(
        functools.partial(kernel, n_outer, n_inner),
        out_shape=(out, out, out),
        in_specs=[pl.BlockSpec(memory_space=pltpu.SMEM)] * 2
        + [pl.BlockSpec(memory_space=pl.ANY)] * 4,
        out_specs=(pl.BlockSpec(memory_space=pltpu.VMEM),) * 3,
        scratch_shapes=scratch,
        compiler_params=pltpu.CompilerParams(
            collective_id=0, has_side_effects=True, vmem_limit_bytes=58 << 20
        ),
    )(chosen, layout, query_vec, key_vec, value_vec, grad_out)


def solution(mesh):
    rows = P(("outer", "inner"), None)
    return jax.shard_map(
        on_device,
        mesh=mesh,
        in_specs=(rows, rows, rows, rows, P(), P()),
        out_specs=(rows, rows, rows),
        check_vma=False,
    )
```

profile of v0, /device:TPU:1, one launch (start us, length us, event | category | flops | bytes accessed | tf_op | source)
XLA Modules:
  0.0 140.0 jit_solution(10995855161995859062)
XLA Ops:
  0.6 1.4 %copy.9.chosen = s32[128,3]{1,0:T(8,128)} copy(s32[128,3]{0,1:T(4,128)} %param.10) | data formatting | bytes 3072 | tf_op args[4]
  2.0 134.0 %shard_map.85 = (bf16[1024,256]{1,0:T(8,128)(2,1)}, bf16[1024,256]{1,0:T(8,128)(2,1)}, bf16[1024,256]{1,0:T(8,128)(2,1)}) custom-call(s32[128,3]{1,0:T(8,128)} %copy.9.chosen, s32[16]{0:T(128)} %layout.1, bf16[1024,256]{1,0:T(8,128)(2,1)} %q_in.1, bf16[1024,256]{1,0:T(8,128)(2,1)} %k_in.1, bf16[1024,256]{1,0:T(8,128)(2,1)} %v_in.1, bf16[1024,256]{1,0:T(8,128)(2,1)} %g_in.1), custom_call_target="tpu_custom_call" | custom-call | tf_op jit(solution)/shard_map/pallas_call | solution.py:291
  136.1 0.0 copy-start.1
  136.1 1.9 %copy.13 = bf16[1024,256]{1,0:T(8,128)(2,1)} copy(bf16[1024,256]{1,0:T(8,128)(2,1)} %get-tuple-element.6) | data formatting | bytes 1048576
  138.0 0.0 copy-done.1
  138.0 0.0 copy-start
  138.0 0.8 copy.14
  138.8 0.4 copy-done
  139.2 0.8 copy.15
Async XLA Ops:
  136.1 1.9 %copy-start.1 = (bf16[1024,256]{1,0:T(8,128)(2,1)S(1)}, bf16[1024,256]{1,0:T(8,128)(2,1)}, u32[]{:S(2)}) copy-start(bf16[1024,256]{1,0:T(8,128)(2,1)} %get-tuple-element.7) | copy-start | bytes 1572868
  138.0 1.2 copy-start
where the time goes:
time: 140 us
  Pallas kernels  134 us (96%)
  local copies, waits for them, and re-layouts  5.37 us (4%)
    pallas_call x1, Pallas kernels, on_device(): pl.pallas_call(functools.partial(kernel, n_outer, n_inner), out_shape=(ou...  134 us
    unnamed x8, local copies, waits for them, and re-layouts  5.37 us

commit v1 on v0

v1 whole, which is shorter than its diff:
```python
import functools
import math

import jax
import jax.numpy as jnp
from jax import lax
from jax.experimental import pallas as pl
from jax.experimental.pallas import tpu as pltpu
from jax.sharding import PartitionSpec as P

HEADS = 2
HD = 128
TOPK = 3
OWN = TOPK
TILE = 16
KEYS = 256
MESH = pl.DeviceIdType.MESH
F32 = jnp.float32
BF16 = jnp.bfloat16
SCALE = 1.0 / math.sqrt(HD)
EXP2_SCALE = SCALE * math.log2(math.e)


def dot(a, b):
    return jnp.dot(a, b, preferred_element_type=F32)


def fold(x, op):
    return op(x.reshape(x.shape[0] // 8, 8, x.shape[1]), axis=0)


def block_rows(ref, h, t, b, base=0):
    return ref[h, t, pl.ds(pl.multiple_of(base + b * KEYS, KEYS), KEYS)]


def causal(shape):
    at = lambda d: lax.broadcasted_iota(jnp.int32, shape, d)
    return at(0) <= at(1)


def own_scores(h, b, qt, kv):
    s = dot(block_rows(kv, h, OWN, b), qt[h, :, b * KEYS :])
    return jnp.where(causal(s.shape), s * EXP2_SCALE, -jnp.inf)


def own_stats(h, qt, gt, kv, s_scr, stats, parts):
    length = qt.shape[2]
    blocks = length // KEYS
    parts[0] = jnp.full((8, length), -jnp.inf, F32)
    parts[1] = jnp.zeros((8, length), F32)
    parts[2] = jnp.zeros((8, length), F32)
    for b in range(blocks):
        s = own_scores(h, b, qt, kv)
        s_scr[b, :, b * KEYS :] = s
        parts[0, :, b * KEYS :] = jnp.maximum(parts[0, :, b * KEYS :], fold(s, jnp.max))
    stats[h, 0:1] = jnp.max(parts[0], axis=0, keepdims=True)
    for b in range(blocks):
        e = jnp.exp2(s_scr[b, :, b * KEYS :] - stats[h, 0:1, b * KEYS :])
        dp = dot(block_rows(kv, h, OWN, b, length), gt[h, :, b * KEYS :])
        parts[1, :, b * KEYS :] += fold(e, jnp.sum)
        parts[2, :, b * KEYS :] += fold(e * dp, jnp.sum)
    stats[h, 1:2] = jnp.sum(parts[1], axis=0, keepdims=True)
    stats[h, 2:3] = jnp.sum(parts[2], axis=0, keepdims=True)


def far_grads(h, picked, q, g, qt, gt, kv, kt, s_scr, dp_scr, stats, dqt, terms):
    length = q.shape[1]
    blocks = length // KEYS
    for t in range(TOPK):
        kt[t] = kv[h, t, :length].T

    def find_max(t, m):
        mt = jnp.full((8, length), -jnp.inf, F32)
        for b in range(blocks):
            s = dot(block_rows(kv, h, t, b), qt[h])
            s_scr[t * blocks + b] = s
            mt = jnp.maximum(mt, fold(s, jnp.max))
        return jnp.maximum(m, jnp.where(picked(t), mt, -jnp.inf))

    m = lax.fori_loop(0, TOPK, find_max, jnp.full((8, length), -jnp.inf, F32))
    own_top = stats[h, 0:1]
    top = jnp.maximum(jnp.max(m, axis=0, keepdims=True) * EXP2_SCALE, own_top)

    def weigh(t, sums):
        total, mixed = sums
        shift = jnp.where(picked(t), top, jnp.inf)
        for b in range(blocks):
            e = jnp.exp2(s_scr[t * blocks + b] * EXP2_SCALE - shift)
            dp = dot(block_rows(kv, h, t, b, length), gt[h])
            s_scr[t * blocks + b] = e
            dp_scr[t * blocks + b] = dp
            total, mixed = total + fold(e, jnp.sum), mixed + fold(e * dp, jnp.sum)
        return total, mixed

    zero = jnp.zeros((8, length), F32)
    total, mixed = lax.fori_loop(0, TOPK, weigh, (zero, zero))
    keep = jnp.exp2(own_top - top)
    total = jnp.sum(total, axis=0, keepdims=True) + stats[h, 1:2] * keep
    inverse = 1.0 / total
    delta = (jnp.sum(mixed, axis=0, keepdims=True) + stats[h, 2:3] * keep) * inverse
    stats[h, 3:4] = top + jnp.log2(total)
    stats[h, 4:5] = delta
    dqt[h] = jnp.zeros(dqt.shape[1:], F32)

    def grads(t, c):
        for b in range(blocks):
            p = s_scr[t * blocks + b] * inverse
            ds = (p * (dp_scr[t * blocks + b] - delta)).astype(BF16)
            rows = pl.ds(b * KEYS, KEYS)
            terms[h, t, rows] = dot(ds, q[h]).astype(BF16)
            terms[h, t, pl.ds(length + b * KEYS, KEYS)] = dot(p.astype(BF16), g[h]).astype(BF16)
            dqt[h] += dot(kt[t, :, rows], ds)
        return c

    lax.fori_loop(0, TOPK, grads, 0)


def own_grads(h, q, g, qt, gt, kv, kt, stats, dqt, dk, dv, gq_ref):
    length = q.shape[1]
    kt[OWN] = kv[h, OWN, :length].T
    for b in range(length // KEYS):
        lanes = slice(b * KEYS, length)
        p = jnp.exp2(own_scores(h, b, qt, kv) - stats[h, 3:4, lanes])
        dp = dot(block_rows(kv, h, OWN, b, length), gt[h, :, lanes])
        ds = (p * (dp - stats[h, 4:5, lanes])).astype(BF16)
        rows = slice(b * KEYS, (b + 1) * KEYS)
        dk[h, rows] = dot(ds, q[h, lanes])
        dv[h, rows] = dot(p.astype(BF16), g[h, lanes])
        dqt[h, :, lanes] += dot(kt[OWN, :, rows], ds)
    gq_ref[:, h * HD : (h + 1) * HD] = (dqt[h].T * SCALE).astype(BF16)


def kernel(
    n_outer, n_inner,
    chosen, layout, q_in, k_in, v_in, g_in,
    gq_ref, gk_ref, gv_ref,
    inverse, wanted, hot_rows, hot, q, g, qt, gt, kv, kt, s_scr, dp_scr, stats, parts, dqt, dk, dv,
    relay0, relay1, outgoing, terms, landed, wide, summed, back,
    in_sem, send_sem, recv_sem,
):
    devices = n_outer * n_inner
    relay = (relay0, relay1)
    my_outer, my_inner = lax.axis_index("outer"), lax.axis_index("inner")
    me = my_outer * n_inner + my_inner
    length = q.shape[1]

    def peer(s):
        o = lax.rem(my_outer + lax.div(s, n_inner), n_outer)
        i = lax.rem(my_inner + lax.rem(s, n_inner), n_inner)
        return o * n_inner + i, (o, i)

    loads = []
    for h in range(HEADS):
        cols = pl.ds(h * HD, HD)
        for src, dst in (
            (k_in, kv.at[h, OWN, pl.ds(0, length)]),
            (v_in, kv.at[h, OWN, pl.ds(length, length)]),
            (q_in, q.at[h]),
            (g_in, g.at[h]),
        ):
            copy = pltpu.make_async_copy(src.at[:, cols], dst, in_sem.at[len(loads)])
            copy.start()
            loads.append(copy)

    barrier = pltpu.get_barrier_semaphore()

    def greet(s, c):
        pl.semaphore_signal(barrier, inc=1, device_id=peer(s)[1], device_id_type=MESH)
        return c

    lax.fori_loop(1, devices, greet, 0)
    for copy in loads:
        copy.wait()

    def exchange(phase, src_of, dst):
        send, recv = send_sem.at[phase], recv_sem.at[phase]
        pltpu.make_async_copy(src_of(me), dst, recv).start()

        def go(s, c):
            r, where = peer(s)
            pltpu.make_async_remote_copy(
                src_ref=src_of(r), dst_ref=dst, send_sem=send, recv_sem=recv,
                device_id=where, device_id_type=MESH,
            ).start()
            return c

        lax.fori_loop(1, devices, go, 0)

    def arrived(phase, whole):
        pltpu.make_async_copy(whole, whole, recv_sem.at[phase]).wait()

    def sent(phase, part):
        pltpu.make_async_copy(part, part, send_sem.at[phase]).wait()

    def place(r):
        return pl.ds(pl.multiple_of(r * TILE, TILE), TILE)

    others = pl.ds(1, devices - 1)

    def spread(h):
        exchange(h, lambda r: kv.at[h, OWN, place(r)], relay[h].at[me])

    def serve(h):
        exchange(2 + h, lambda r: outgoing.at[h, r], kv.at[h, pl.ds(0, TOPK), place(me)])

    def pick(h):
        arrived(h, relay[h])

        def one(r, c):
            for t in range(TOPK):
                outgoing[h, r, t] = relay[h][wanted[r * TOPK + t]]
            return c

        lax.fori_loop(0, devices, one, 0)

    def work(h):
        arrived(2 + h, kv.at[h, pl.ds(0, TOPK)])
        far_grads(h, picked, q, g, qt, gt, kv, kt, s_scr, dp_scr, stats, dqt, terms)
        exchange(4 + h, lambda r: terms.at[h, :, place(r)], landed.at[h, me])

    def add_up(h):
        arrived(4 + h, landed.at[h])

        def widen(r, c):
            wide[pl.ds(r * TOPK * TILE, TOPK * TILE)] = (
                landed[h, r].astype(F32).reshape(TOPK * TILE, HD)
            )
            return c

        lax.fori_loop(0, devices, widen, 0)
        sums = []
        for s in range(TILE):
            part = wide[pl.ds(s, devices * TOPK, TILE), :].astype(BF16)
            sums.append(dot(hot[...], part))
        for s in range(TILE):
            wide[pl.ds(s, devices, TILE), :] = sums[s]
        summed[h] = wide[: devices * TILE].astype(BF16)
        exchange(6 + h, lambda r: summed.at[h, place(r)], back.at[h, place(me)])

    def finish(h):
        arrived(6 + h, back.at[h])
        cols = pl.ds(h * HD, HD)
        gk_ref[:, cols] = ((dk[h] + back[h, :length].astype(F32)) * SCALE).astype(BF16)
        gv_ref[:, cols] = (dv[h] + back[h, length:].astype(F32)).astype(BF16)

    pl.semaphore_wait(barrier, devices - 1)
    spread(0)

    def invert(p, c):
        inverse[p] = sum(jnp.where(layout[j] == p, j, 0) for j in range(n_inner))
        return c

    lax.fori_loop(0, n_inner, invert, 0)
    lane = lax.broadcasted_iota(jnp.int32, (1, devices), 1)

    def want(r, c):
        block = lax.div(r, n_inner) * n_inner + layout[lax.rem(r, n_inner)]
        for t in range(TOPK):
            row = chosen[t, block]
            row = lax.div(row, n_inner) * n_inner + inverse[lax.rem(row, n_inner)]
            wanted[r * TOPK + t] = row
            hot_rows[pl.ds(r * TOPK + t, 1), :] = jnp.where(lane == row, 1.0, 0.0)
        return c

    lax.fori_loop(0, devices, want, 0)
    my_block = my_outer * n_inner + layout[my_inner]

    def picked(t):
        return chosen[t, my_block] < my_block

    sent(0, relay[0].at[others])
    spread(1)
    hot[...] = hot_rows[...].T.astype(BF16)
    for h in range(HEADS):
        qt[h] = q[h].T
        gt[h] = g[h].T
    pick(0)
    serve(0)
    for h in range(HEADS):
        own_stats(h, qt, gt, kv, s_scr, stats, parts)
    pick(1)
    sent(2, outgoing.at[0, others])
    serve(1)
    work(0)
    work(1)
    for h in range(HEADS):
        own_grads(h, q, g, qt, gt, kv, kt, stats, dqt, dk, dv, gq_ref)
        add_up(h)
    for h in range(HEADS):
        finish(h)
    sent(1, relay[1].at[others])
    sent(3, outgoing.at[1, others])
    for h in range(HEADS):
        sent(4 + h, landed.at[h, others])
        sent(6 + h, summed.at[h, pl.ds(TILE, (devices - 1) * TILE)])


def on_device(query_vec, key_vec, value_vec, grad_out, chosen, layout):
    n_outer, n_inner = lax.axis_size("outer"), lax.axis_size("inner")
    devices = n_outer * n_inner
    length, width = query_vec.shape
    blocks = length // KEYS
    out = jax.ShapeDtypeStruct((length, width), BF16)
    scratch = [
        pltpu.SMEM((n_inner,), jnp.int32),
        pltpu.SMEM((devices * TOPK,), jnp.int32),
        pltpu.VMEM((devices * TOPK, devices), F32),
        pltpu.VMEM((devices, devices * TOPK), BF16),
        pltpu.VMEM((HEADS, length, HD), BF16),
        pltpu.VMEM((HEADS, length, HD), BF16),
        pltpu.VMEM((HEADS, HD, length), BF16),
        pltpu.VMEM((HEADS, HD, length), BF16),
        pltpu.VMEM((HEADS, TOPK + 1, 2 * length, HD), BF16),
        pltpu.VMEM((TOPK + 1, HD, length), BF16),
        pltpu.VMEM((TOPK * blocks, KEYS, length), F32),
        pltpu.VMEM((TOPK * blocks, KEYS, length), F32),
        pltpu.VMEM((HEADS, 8, length), F32),
        pltpu.VMEM((3, 8, length), F32),
        pltpu.VMEM((HEADS, HD, length), F32),
        pltpu.VMEM((HEADS, length, HD), F32),
        pltpu.VMEM((HEADS, length, HD), F32),
        pltpu.VMEM((devices, TILE, HD), BF16),
        pltpu.VMEM((devices, TILE, HD), BF16),
        pltpu.VMEM((HEADS, devices, TOPK, TILE, HD), BF16),
        pltpu.VMEM((HEADS, TOPK, 2 * length, HD), BF16),
        pltpu.VMEM((HEADS, devices, TOPK, TILE, HD), BF16),
        pltpu.VMEM((devices * TOPK * TILE, HD), F32),
        pltpu.VMEM((HEADS, devices * TILE, HD), BF16),
        pltpu.VMEM((HEADS, devices * TILE, HD), BF16),
        pltpu.SemaphoreType.DMA((4 * HEADS,)),
        pltpu.SemaphoreType.DMA((4 * HEADS,)),
        pltpu.SemaphoreType.DMA((4 * HEADS,)),
    ]
    return pl.pallas_call(
        functools.partial(kernel, n_outer, n_inner),
        out_shape=(out, out, out),
        in_specs=[pl.BlockSpec(memory_space=pltpu.SMEM)] * 2
        + [pl.BlockSpec(memory_space=pl.ANY)] * 4,
        out_specs=(pl.BlockSpec(memory_space=pltpu.VMEM),) * 3,
        scratch_shapes=scratch,
        compiler_params=pltpu.CompilerParams(
            collective_id=0, has_side_effects=True, vmem_limit_bytes=58 << 20
        ),
    )(chosen.T, layout, query_vec, key_vec, value_vec, grad_out)


def solution(mesh):
    rows = P(("outer", "inner"), None)
    return jax.shard_map(
        on_device,
        mesh=mesh,
        in_specs=(rows, rows, rows, rows, P(), P()),
        out_specs=(rows, rows, rows),
        check_vma=False,
    )
```

time: 140 us -> 121 us (0.86)
  Pallas kernels: 134 us -> 116 us
  local copies, waits for them, and re-layouts: 5.37 us -> 3.95 us
    pallas_call x1, Pallas kernels: 134 us -> 116 us  [on_device(): pl.pallas_call(functools.partial(kernel, n_outer, n_inner), out_shape=(ou...]
    unnamed x8 -> x7, local copies, waits for them, and re-layouts: 5.37 us -> 3.95 us
where the time goes in v1:
time: 121 us
  Pallas kernels  116 us (96%)
  local copies, waits for them, and re-layouts  3.95 us (3%)
    pallas_call x1, Pallas kernels, on_device(): pl.pallas_call(functools.partial(kernel, n_outer, n_inner), out_shape=(ou...  116 us
    unnamed x7, local copies, waits for them, and re-layouts  3.95 us

profile of v1, /device:TPU:1, one launch (start us, length us, event | category | flops | bytes accessed | tf_op | source)
XLA Modules:
  0.0 121.0 jit_solution(8716808268002204210)
XLA Ops:
  0.6 116.4 %shard_map.85 = (bf16[1024,256]{1,0:T(8,128)(2,1)}, bf16[1024,256]{1,0:T(8,128)(2,1)}, bf16[1024,256]{1,0:T(8,128)(2,1)}) custom-call(s32[3,128]{1,0:T(4,128)} %bitcast.1, s32[16]{0:T(128)} %layout.1, bf16[1024,256]{1,0:T(8,128)(2,1)} %q_in.1, bf16[1024,256]{1,0:T(8,128)(2,1)} %k_in.1, bf16[1024,256]{1,0:T(8,128)(2,1)} %v_in.1, bf16[1024,256]{1,0:T(8,128)(2,1)} %g_in.1), custom_call_target="tpu_custom_call" | custom-call | tf_op jit(solution)/shard_map/pallas_call | solution.py:334
  117.0 0.0 copy-start.1
  117.1 1.9 %copy.12 = bf16[1024,256]{1,0:T(8,128)(2,1)} copy(bf16[1024,256]{1,0:T(8,128)(2,1)} %get-tuple-element.6) | data formatting | bytes 1048576
  119.0 0.0 copy-done.1
  119.0 0.0 copy-start
  119.0 0.8 copy.13
  119.8 0.4 copy-done
  120.2 0.8 copy.14
Async XLA Ops:
  117.0 1.9 %copy-start.1 = (bf16[1024,256]{1,0:T(8,128)(2,1)S(1)}, bf16[1024,256]{1,0:T(8,128)(2,1)}, u32[]{:S(2)}) copy-start(bf16[1024,256]{1,0:T(8,128)(2,1)} %get-tuple-element.7) | copy-start | bytes 1572868
  119.0 1.2 %copy-start = (bf16[1024,256]{1,0:T(8,128)(2,1)S(1)}, bf16[1024,256]{1,0:T(8,128)(2,1)}, u32[]{:S(2)}) copy-start(bf16[1024,256]{1,0:T(8,128)(2,1)} %get-tuple-element.8) | copy-start | bytes 1572868

commit v2 on v1

--- a/solution.py
+++ b/solution.py
@@ -14,6 +14,7 @@
 OWN = TOPK
 TILE = 16
 KEYS = 256
+PARTS = 2
 MESH = pl.DeviceIdType.MESH
 F32 = jnp.float32
 BF16 = jnp.bfloat16
@@ -144,10 +145,14 @@
     me = my_outer * n_inner + my_inner
     length = q.shape[1]
 
-    def peer(s):
-        o = lax.rem(my_outer + lax.div(s, n_inner), n_outer)
-        i = lax.rem(my_inner + lax.rem(s, n_inner), n_inner)
-        return o * n_inner + i, (o, i)
+    def each_peer(act):
+        def one(s, c):
+            o = lax.rem(my_outer + lax.div(s, n_inner), n_outer)
+            i = lax.rem(my_inner + lax.rem(s, n_inner), n_inner)
+            act(o * n_inner + i, (o, i))
+            return c
+
+        lax.fori_loop(1, devices, one, 0)
 
     loads = []
     for h in range(HEADS):
@@ -164,11 +169,11 @@
 
     barrier = pltpu.get_barrier_semaphore()
 
-    def greet(s, c):
-        pl.semaphore_signal(barrier, inc=1, device_id=peer(s)[1], device_id_type=MESH)
-        return c
-
-    lax.fori_loop(1, devices, greet, 0)
+    each_peer(
+        lambda r, where: pl.semaphore_signal(
+            barrier, inc=1, device_id=where, device_id_type=MESH
+        )
+    )
     for copy in loads:
         copy.wait()
 
@@ -176,15 +181,13 @@
         send, recv = send_sem.at[phase], recv_sem.at[phase]
         pltpu.make_async_copy(src_of(me), dst, recv).start()
 
-        def go(s, c):
-            r, where = peer(s)
+        def send_one(r, where):
             pltpu.make_async_remote_copy(
                 src_ref=src_of(r), dst_ref=dst, send_sem=send, recv_sem=recv,
                 device_id=where, device_id_type=MESH,
             ).start()
-            return c
-
-        lax.fori_loop(1, devices, go, 0)
+
+        each_peer(send_one)
 
     def arrived(phase, whole):
         pltpu.make_async_copy(whole, whole, recv_sem.at[phase]).wait()
@@ -235,6 +238,8 @@
         for s in range(TILE):
             wide[pl.ds(s, devices, TILE), :] = sums[s]
         summed[h] = wide[: devices * TILE].astype(BF16)
+
+    def bring_home(h):
         exchange(6 + h, lambda r: summed.at[h, place(r)], back.at[h, place(me)])
 
     def finish(h):
@@ -268,7 +273,6 @@
     def picked(t):
         return chosen[t, my_block] < my_block
 
-    sent(0, relay[0].at[others])
     spread(1)
     hot[...] = hot_rows[...].T.astype(BF16)
     for h in range(HEADS):
@@ -285,14 +289,24 @@
     work(1)
     for h in range(HEADS):
         own_grads(h, q, g, qt, gt, kv, kt, stats, dqt, dk, dv, gq_ref)
-        add_up(h)
+    add_up(0)
+    sent(5, landed.at[1, others])
+    bring_home(0)
+    add_up(1)
+    bring_home(1)
     for h in range(HEADS):
         finish(h)
+    sent(0, relay[0].at[others])
     sent(1, relay[1].at[others])
     sent(3, outgoing.at[1, others])
-    for h in range(HEADS):
-        sent(4 + h, landed.at[h, others])
+    sent(4, landed.at[0, others])
+    for h in range(HEADS):
         sent(6 + h, summed.at[h, pl.ds(TILE, (devices - 1) * TILE)])
+
+
+def hand_on(*refs):
+    for source, target in zip(refs[:3], refs[3:]):
+        target[...] = source[...]
 
 
 def on_device(query_vec, key_vec, value_vec, grad_out, chosen, layout):
@@ -331,7 +345,7 @@
         pltpu.SemaphoreType.DMA((4 * HEADS,)),
         pltpu.SemaphoreType.DMA((4 * HEADS,)),
     ]
-    return pl.pallas_call(
+    results = pl.pallas_call(
         functools.partial(kernel, n_outer, n_inner),
         out_shape=(out, out, out),
         in_specs=[pl.BlockSpec(memory_space=pltpu.SMEM)] * 2
@@ -342,6 +356,13 @@
             collective_id=0, has_side_effects=True, vmem_limit_bytes=58 << 20
         ),
     )(chosen.T, layout, query_vec, key_vec, value_vec, grad_out)
+    return pl.pallas_call(
+        hand_on,
+        out_shape=(out, out, out),
+        grid=(PARTS,),
+        in_specs=[pl.BlockSpec((length // PARTS, width), lambda p: (p, 0))] * 3,
+        out_specs=(pl.BlockSpec((length // PARTS, width), lambda p: (p, 0)),) * 3,
+    )(*results)
 
 
 def solution(mesh):

time: 121 us -> 116 us (0.959)
  local copies, waits for them, and re-layouts: 3.95 us -> 0 us
    unnamed x7 -> x0, local copies, waits for them, and re-layouts: 3.95 us -> none
    pallas_call x1, Pallas kernels: 116 us -> 113 us  [on_device(): pl.pallas_call(functools.partial(kernel, n_outer, n_inner), out_shape=(ou...]
    pallas_call x0 -> x1, Pallas kernels: none -> 2.31 us  [on_device(): pl.pallas_call(hand_on, out_shape=(out, out, out), grid=(PARTS,), in_spec...]
where the time goes in v2:
time: 116 us; the launch traced here: 115 us
  Pallas kernels  115 us (99%)
    pallas_call x1, Pallas kernels, on_device(): pl.pallas_call(functools.partial(kernel, n_outer, n_inner), out_shape=(ou...  113 us

profile of v2, /device:TPU:1, one launch (start us, length us, event | category | flops | bytes accessed | tf_op | source)
XLA Modules:
  0.0 115.5 jit_solution(6416691103407823055)
XLA Ops:
  0.6 112.5 %shard_map.85 = (bf16[1024,256]{1,0:T(8,128)(2,1)}, bf16[1024,256]{1,0:T(8,128)(2,1)}, bf16[1024,256]{1,0:T(8,128)(2,1)}) custom-call(s32[3,128]{1,0:T(4,128)} %bitcast.1, s32[16]{0:T(128)} %layout.1, bf16[1024,256]{1,0:T(8,128)(2,1)} %q_in.1, bf16[1024,256]{1,0:T(8,128)(2,1)} %k_in.1, bf16[1024,256]{1,0:T(8,128)(2,1)} %v_in.1, bf16[1024,256]{1,0:T(8,128)(2,1)} %g_in.1), custom_call_target="tpu_custom_call" | custom-call | tf_op jit(solution)/shard_map/pallas_call | solution.py:348
  113.2 2.3 %shard_map.86 = (bf16[1024,256]{1,0:T(8,128)(2,1)}, bf16[1024,256]{1,0:T(8,128)(2,1)}, bf16[1024,256]{1,0:T(8,128)(2,1)}) custom-call(bf16[1024,256]{1,0:T(8,128)(2,1)} %get-tuple-element.6.refs_0_, bf16[1024,256]{1,0:T(8,128)(2,1)} %get-tuple-element.7.refs_1_, bf16[1024,256]{1,0:T(8,128)(2,1)} %get-tuple-element.8.refs_2_), custom_call_target="tpu_custom_call" | custom-call | tf_op jit(solution)/shard_map/pallas_call | solution.py:359

commit v3 on v2

--- a/solution.py
+++ b/solution.py
@@ -145,14 +145,16 @@
     me = my_outer * n_inner + my_inner
     length = q.shape[1]
 
-    def each_peer(act):
+    def each_peer(act, start=1):
         def one(s, c):
             o = lax.rem(my_outer + lax.div(s, n_inner), n_outer)
             i = lax.rem(my_inner + lax.rem(s, n_inner), n_inner)
             act(o * n_inner + i, (o, i))
             return c
 
-        lax.fori_loop(1, devices, one, 0)
+        lax.fori_loop(start, devices, one, 0)
+        if start > 1:
+            lax.fori_loop(1, start, one, 0)
 
     loads = []
     for h in range(HEADS):
@@ -187,7 +189,7 @@
                 device_id=where, device_id_type=MESH,
             ).start()
 
-        each_peer(send_one)
+        each_peer(send_one, 2 * n_inner if phase >= 6 else 1)
 
     def arrived(phase, whole):
         pltpu.make_async_copy(whole, whole, recv_sem.at[phase]).wait()

time: 116 us -> 115 us (level)
  no operation moved by 1% of the time
where the time goes in v3:
time: 115 us
  Pallas kernels  115 us (100%)
    pallas_call x1, Pallas kernels, on_device(): pl.pallas_call(functools.partial(kernel, n_outer, n_inner), out_shape=(ou...  112 us
    pallas_call x1, Pallas kernels, on_device(): pl.pallas_call(hand_on, out_shape=(out, out, out), grid=(PARTS,), in_spec...  2.31 us

profile of v3, /device:TPU:1, one launch (start us, length us, event | category | flops | bytes accessed | tf_op | source)
XLA Modules:
  0.0 115.2 jit_solution(16980371099735309271)
XLA Ops:
  0.6 112.3 %shard_map.85 = (bf16[1024,256]{1,0:T(8,128)(2,1)}, bf16[1024,256]{1,0:T(8,128)(2,1)}, bf16[1024,256]{1,0:T(8,128)(2,1)}) custom-call(s32[3,128]{1,0:T(4,128)} %bitcast.1, s32[16]{0:T(128)} %layout.1, bf16[1024,256]{1,0:T(8,128)(2,1)} %q_in.1, bf16[1024,256]{1,0:T(8,128)(2,1)} %k_in.1, bf16[1024,256]{1,0:T(8,128)(2,1)} %v_in.1, bf16[1024,256]{1,0:T(8,128)(2,1)} %g_in.1), custom_call_target="tpu_custom_call" | custom-call | tf_op jit(solution)/shard_map/pallas_call | solution.py:350
  112.9 2.3 %shard_map.86 = (bf16[1024,256]{1,0:T(8,128)(2,1)}, bf16[1024,256]{1,0:T(8,128)(2,1)}, bf16[1024,256]{1,0:T(8,128)(2,1)}) custom-call(bf16[1024,256]{1,0:T(8,128)(2,1)} %get-tuple-element.6.refs_0_, bf16[1024,256]{1,0:T(8,128)(2,1)} %get-tuple-element.7.refs_1_, bf16[1024,256]{1,0:T(8,128)(2,1)} %get-tuple-element.8.refs_2_), custom_call_target="tpu_custom_call" | custom-call | tf_op jit(solution)/shard_map/pallas_call | solution.py:361
